TPU v7x, 512 devices: a whole 4x4x16 slice. The times are simulated.
512 devices in a mesh: seq: 32 (over y_hi, z), head: 16 (over y_lo, x, core).
Axes of the slice: x: 4, y: 4 (y_hi: 2, y_lo: 2; y = y_hi * 2 + y_lo), z: 16, core: 2. Of those that a mesh axis runs over, the one named last changes fastest.
Arguments:
- queries: bfloat16 [8192, 6144], P('seq', 'head'), may hold values from -42 to 42
- keys: bfloat16 [8192, 6144], P('seq', 'head'), may hold values from -4 to 4
- values: bfloat16 [8192, 6144], P('seq', 'head'), may hold values from -120 to 120
- block_mask: int32 [64, 64], P('seq'), may hold values from 0 to 1
- region_of_block: int32 [64], P('seq'), may hold values from 0 to 7
- text_keys: bfloat16 [8, 256, 6144], P(None, 'seq', 'head'), may hold values from -4 to 4
- text_values: bfloat16 [8, 256, 6144], P(None, 'seq', 'head'), may hold values from -6 to 6
- gain: bfloat16 [6144], P('head'), may hold values from 0.099609375 to 1.8984375
Outputs:
- mixed: bfloat16 [8192, 6144], P('seq', 'head')
All inputs are finite; a program needn't handle non-finite values.
Results may differ from a plain program's by a relative error of at most 0.0085.
Values may be sent and summed in bfloat16 or wider, within the bound.
A program may use at most 64 MiB of HBM per device.

v0:
```python
import jax
import jax.numpy as jnp
from jax import lax
from jax.sharding import PartitionSpec as P

HEADS = 48
HD = 128
BLK = 128
TXT = 256


def absorb(carry, query_rows, key_block, value_block, tile, softmax_scale):
    top, total, accum = carry
    keep = jnp.repeat(jnp.repeat(tile, BLK, axis=0), BLK, axis=1)
    scores = (
        jnp.einsum("qhd,khd->hqk", query_rows, key_block, preferred_element_type=jnp.float32)
        * softmax_scale
    )
    scores = jnp.where(keep[None], scores, -1e30)
    new_top = jnp.maximum(top, jnp.max(scores, axis=-1))
    weights = jnp.where(keep[None], jnp.exp(scores - new_top[..., None]), 0.0)
    factor = jnp.exp(top - new_top)
    total = total * factor + jnp.sum(weights, axis=-1)
    update = jnp.einsum(
        "hqk,khd->hqd",
        weights.astype(jnp.bfloat16),
        value_block,
        preferred_element_type=jnp.float32,
    )
    accum = accum * factor[..., None] + update
    return (new_top, total, accum)


def local(queries, keys, values, block_mask, region_of_block, text_keys, text_values, gain):
    tok, width = queries.shape
    heads = width // HD
    blocks = tok // BLK
    softmax_scale = HD ** (-0.5)
    first = lax.axis_index("seq") * blocks
    columns = jnp.arange(block_mask.shape[1], dtype=jnp.int32)
    owned = first + jnp.arange(blocks, dtype=jnp.int32)
    allowed = (block_mask > 0) | (columns[None, :] == owned[:, None])
    query_rows = queries.reshape(tok, heads, HD)
    start_state = (
        jnp.full((heads, tok), -1e30, jnp.float32),
        jnp.zeros((heads, tok), jnp.float32),
        jnp.zeros((heads, tok, HD), jnp.float32),
    )
    key_piece = lax.all_gather(keys, "seq", axis=0, tiled=True)
    value_piece = lax.all_gather(values, "seq", axis=0, tiled=True)
    rows = key_piece.shape[0]
    stride = 2 * tok

    def inner(index, carry):
        offset = index * stride
        key_block = lax.dynamic_slice_in_dim(key_piece, offset, stride, 0).reshape(
            stride, heads, HD
        )
        value_block = lax.dynamic_slice_in_dim(value_piece, offset, stride, 0).reshape(
            stride, heads, HD
        )
        tile = lax.dynamic_slice_in_dim(allowed, offset // BLK, stride // BLK, 1)
        return absorb(carry, query_rows, key_block, value_block, tile, softmax_scale)

    state = lax.fori_loop(0, rows // stride, inner, start_state)
    region_panel_key_rows, region_panel_value_rows = (
        lax.all_gather(text_keys, "seq", axis=1, tiled=True),
        lax.all_gather(text_values, "seq", axis=1, tiled=True),
    )
    top, total, accum = state
    self_out = jnp.transpose(accum / total[..., None], (1, 0, 2)).reshape(tok, width)
    chosen_keys = region_panel_key_rows[region_of_block].reshape(blocks, TXT, heads, HD)
    chosen_values = region_panel_value_rows[region_of_block].reshape(blocks, TXT, heads, HD)
    query_block_groups = queries.reshape(blocks, BLK, heads, HD)
    caption_score_matrix = (
        jnp.einsum(
            "bqhd,bthd->bhqt", query_block_groups, chosen_keys, preferred_element_type=jnp.float32
        )
        * softmax_scale
    )
    text_top = jnp.max(caption_score_matrix, axis=-1, keepdims=True)
    text_weights = jnp.exp(caption_score_matrix - text_top)
    caption_score_sum = jnp.sum(text_weights, axis=-1)
    cross_sum = jnp.einsum(
        "bhqt,bthd->bqhd",
        text_weights.astype(jnp.bfloat16),
        chosen_values,
        preferred_element_type=jnp.float32,
    )
    cross_out = (cross_sum / jnp.transpose(caption_score_sum, (0, 2, 1))[..., None]).reshape(
        tok, width
    )
    combined = self_out + cross_out
    squares = jnp.sum(combined * combined, axis=1)
    square_total = lax.psum(squares, "head")
    mean_square = square_total / (HEADS * HD)
    scaled = combined * lax.rsqrt(mean_square + 1e-06)[:, None] * gain.astype(jnp.float32)[None, :]
    return scaled.astype(jnp.bfloat16)


def solution(mesh):
    in_specs = (
        P("seq", "head"),
        P("seq", "head"),
        P("seq", "head"),
        P("seq", None),
        P("seq"),
        P(None, "seq", "head"),
        P(None, "seq", "head"),
        P("head"),
    )
    out_specs = P("seq", "head")
    return jax.shard_map(local, mesh=mesh, in_specs=in_specs, out_specs=out_specs, check_vma=False)
```

profile of v0, /device:TPU:1, one launch (start us, length us, event | category | flops | bytes accessed | tf_op | source)
XLA Modules:
  0.0 747.4 jit_solution(13527715328726537299)
XLA Ops:
  6.6 0.7 all-gather.11.cloned.1.call-update
  7.3 0.7 all-gather.9.cloned.1.call-update
  8.1 1.7 copy.37
  9.9 1.7 copy.39
  11.6 1.0 reshape.95
  13.2 133.5 %all-gather.11.cloned.1.call-done = bf16[8,256,384]{2,1,0:T(8,128)(2,1)} async-done(((bf16[8,8,384]{2,1,0:T(8,128)(2,1)}), bf16[8,256,384]{2,1,0:T(8,128)(2,1)}) %all-gather.11.cloned.1.call-update) | async-done | bytes 1572880 | tf_op jit(solution)/shard_map/all_gather | solution.py:67
  146.7 2.0 gather_fusion.1
  148.9 135.7 %all-gather.9.cloned.1.call-done = bf16[8,256,384]{2,1,0:T(8,128)(2,1)} async-done(((bf16[8,8,384]{2,1,0:T(8,128)(2,1)}), bf16[8,256,384]{2,1,0:T(8,128)(2,1)}) %all-gather.9.cloned.1.call-update) | async-done | bytes 1572880 | tf_op jit(solution)/shard_map/all_gather | solution.py:68
  284.6 2.0 gather_fusion
  288.1 183.3 %all-gather.5.cloned.1.call-done = bf16[8192,384]{0,1:T(8,128)(2,1)} async-done(((bf16[256,384]{0,1:T(8,128)(2,1)}), bf16[8192,384]{0,1:T(8,128)(2,1)}) %all-gather.5.cloned.1.call-update) | async-done | bytes 6291472 | tf_op jit(solution)/shard_map/all_gather | solution.py:49
  471.4 185.5 %all-gather.7.cloned.1.call-done = bf16[8192,384]{0,1:T(8,128)(2,1)} async-done(((bf16[256,384]{0,1:T(8,128)(2,1)}), bf16[8192,384]{0,1:T(8,128)(2,1)}) %all-gather.7.cloned.1.call-update) | async-done | bytes 6291472 | tf_op jit(solution)/shard_map/all_gather | solution.py:50
  656.8 46.9 %while.20 = (s32[]{:T(128)}, f32[3,256]{1,0:T(4,128)S(1)}, f32[3,256]{1,0:T(4,128)S(1)}, f32[3,256,128]{2,1,0:T(8,128)S(1)}, pred[2,64]{1,0:T(4,128)(4,1)S(1)}, ...) while((s32[]{:T(128)}, f32[3,256]{1,0:T(4,128)S(1)}, ...), condition=%wide.region_3.4_spmd.clone, body=%wide.region_0.3_spmd.clone.sunk | while | flops 205164320 | bytes 8636830 | solution.py:65
  657.0 1.2 constant_dynamic-slice_fusion.5
  659.1 0.6 convolution_add_fusion.2
  660.0 1.2 constant_dynamic-slice_fusion.5
  662.0 0.6 convolution_add_fusion.2
  662.9 1.2 constant_dynamic-slice_fusion.5
  665.9 1.2 constant_dynamic-slice_fusion.5
  668.8 1.2 constant_dynamic-slice_fusion.5
  671.7 1.2 constant_dynamic-slice_fusion.5
  674.7 1.2 constant_dynamic-slice_fusion.5
  677.6 1.2 constant_dynamic-slice_fusion.5
  680.5 1.2 constant_dynamic-slice_fusion.5
  683.5 1.2 constant_dynamic-slice_fusion.5
  686.4 1.2 constant_dynamic-slice_fusion.5
  689.3 1.2 constant_dynamic-slice_fusion.5
  692.3 1.2 constant_dynamic-slice_fusion.5
  695.2 1.2 constant_dynamic-slice_fusion.5
  698.1 1.2 constant_dynamic-slice_fusion.5
  701.1 1.2 constant_dynamic-slice_fusion.5
  704.0 35.9 %psum.7 = f32[256]{0:T(256)S(1)} all-reduce(f32[256]{0:T(256)S(1)} %get-tuple-element.268), channel_id=1, replica_groups=mesh['seq'=32,'head'=16] {'head'}, use_global_device_ids=true, to_apply=%region_7.8 | all-reduce | flops 256 | bytes 2048 | tf_op jit(solution)/shard_map/psum | solution.py:95
  740.1 0.8 copy.52
  (178 shorter events, 28.0 us)
Async XLA Ops:
  6.5 6.1 copy-start
  6.5 6.5 copy-start.1
  6.5 6.5 copy-start.3
  6.5 6.5 copy-start.2
  6.5 140.1 %all-gather.11.cloned.1.call-start = ((), (), s32[]{:S(2)}) async-start(), calls=%async_computation.3 | async-start | bytes 1622016 | tf_op jit(solution)/shard_map/all_gather | solution.py:67
  7.3 277.3 %all-gather.9.cloned.1.call-start = ((), (), s32[]{:S(2)}) async-start(), calls=%async_computation.2 | async-start | bytes 1622016 | tf_op jit(solution)/shard_map/all_gather | solution.py:68
  8.0 463.4 %all-gather.5.cloned.1.call-start = ((), (), s32[]{:S(2)}) async-start(), calls=%async_computation | async-start | bytes 6488064 | tf_op jit(solution)/shard_map/all_gather | solution.py:49
  9.8 647.0 %all-gather.7.cloned.1.call-start = ((), (), s32[]{:S(2)}) async-start(), calls=%async_computation.1 | async-start | bytes 6488064 | tf_op jit(solution)/shard_map/all_gather | solution.py:50
Sparse Core Ops, SparseCore 0:
  10.3 136.3 all-gather.10
  149.6 134.9 all-gather.8
  287.5 183.8 all-gather.4
  474.1 182.6 all-gather.6
where the time goes:
time: 748 us; the launch traced here: 747 us
  waiting for transfers between devices  639 us (85%)
  blocking collectives  35.9 us (5%)
  local copies, waits for them, and re-layouts  32.6 us (4%)
  matrix products  18.8 us (3%)
  between operations  13.3 us (2%)
    all_gather x1, waiting for transfers between devices, local(): value_piece = lax.all_gather(values, 'seq', axis=0, tiled=True)  185 us
    all_gather x1, waiting for transfers between devices, local(): key_piece = lax.all_gather(keys, 'seq', axis=0, tiled=True)  183 us
    all_gather x1, waiting for transfers between devices, local(): lax.all_gather(text_values, 'seq', axis=1, tiled=True)  136 us
    all_gather x1, waiting for transfers between devices, local(): lax.all_gather(text_keys, 'seq', axis=1, tiled=True)  134 us
    psum x1, blocking collectives, local(): square_total = lax.psum(squares, 'head')  35.9 us
    dynamic_slice x16, local copies, waits for them, and re-layouts, inner(): lax.dynamic_slice_in_dim(value_piece, offset, stride, 0)  18.8 us
  transfers between devices with their start and end apart: 4, of which 4 were waited for; matrix products, arithmetic and copies ran while one was open for 1% of the time, Pallas kernels for 0%

commit v1 on v0

--- a/solution.py
+++ b/solution.py
@@ -7,6 +7,11 @@
 HD = 128
 BLK = 128
 TXT = 256
+
+
+def all_by_exchange(value, mesh_axis, along):
+    outgoing = jnp.stack([value] * lax.axis_size(mesh_axis))
+    return jnp.concatenate(lax.all_to_all(outgoing, mesh_axis, 0, 0), axis=along)
 
 
 def absorb(carry, query_rows, key_block, value_block, tile, softmax_scale):
@@ -64,7 +69,7 @@
 
     state = lax.fori_loop(0, rows // stride, inner, start_state)
     region_panel_key_rows, region_panel_value_rows = (
-        lax.all_gather(text_keys, "seq", axis=1, tiled=True),
+        all_by_exchange(text_keys, "seq", 1),
         lax.all_gather(text_values, "seq", axis=1, tiled=True),
     )
     top, total, accum = state

time: 748 us -> 646 us (0.86)
  waiting for transfers between devices: 639 us -> 516 us
  starting transfers between devices: 0.15 us -> 18.9 us
    all_gather x1 -> x0, waiting for transfers between devices: 134 us -> none  [local(): lax.all_gather(text_keys, 'seq', axis=1, tiled=True)]
    all_to_all x0 -> x1, starting transfers between devices: none -> 18.8 us  [all_by_exchange(): lax.all_to_all(outgoing, mesh_axis, 0, 0)]
    all_gather x1, waiting for transfers between devices: 136 us -> 150 us  [local(): lax.all_gather(text_values, 'seq', axis=1, tiled=True)]
  transfers between devices with their start and end apart: 4 -> 4, of which waited for: 4 -> 3; matrix products, arithmetic and copies ran while one was open for 1% -> 2% of each run, Pallas kernels for 0% -> 0%
where the time goes in v1:
time: 646 us
  waiting for transfers between devices  516 us (80%)
  blocking collectives  35.9 us (6%)
  local copies, waits for them, and re-layouts  35.2 us (5%)
  matrix products  19.1 us (3%)
  starting transfers between devices  18.9 us (3%)
  between operations  13.3 us (2%)
    all_gather x1, waiting for transfers between devices, local(): value_piece = lax.all_gather(values, 'seq', axis=0, tiled=True)  186 us
    all_gather x1, waiting for transfers between devices, local(): key_piece = lax.all_gather(keys, 'seq', axis=0, tiled=True)  180 us
    all_gather x1, waiting for transfers between devices, local(): lax.all_gather(text_values, 'seq', axis=1, tiled=True)  150 us
    psum x1, blocking collectives, local(): square_total = lax.psum(squares, 'head')  35.9 us
    dynamic_slice x16, local copies, waits for them, and re-layouts, inner(): lax.dynamic_slice_in_dim(value_piece, offset, stride, 0)  18.8 us
    all_to_all x1, starting transfers between devices, all_by_exchange(): lax.all_to_all(outgoing, mesh_axis, 0, 0)  18.8 us
  transfers between devices with their start and end apart: 4, of which 3 were waited for; matrix products, arithmetic and copies ran while one was open for 2% of the time, Pallas kernels for 0%

profile of v1, /device:TPU:1, one launch (start us, length us, event | category | flops | bytes accessed | tf_op | source)
XLA Modules:
  0.0 645.7 jit_solution(16096994445094133896)
XLA Ops:
  6.5 0.7 all-gather.8.cloned.1.call-update
  7.3 1.7 copy.56
  9.1 1.8 copy.58
  10.9 2.2 stack.2
  13.1 18.8 %all-to-all-start = ((bf16[32,8,8,384]{3,2,1,0:T(8,128)(2,1)}), bf16[32,8,8,384]{3,2,1,0:T(8,128)(2,1)S(1)}, u32[]{:S(2)}, u32[]{:S(2)}) async-start(bf16[32,8,8,384]{3,2,1,0:T(8,128)(2,1)} %stack.2), calls=%async_computation | async-start | bytes 3145728 | tf_op jit(solution)/shard_map/all_to_all | solution.py:14
  32.5 150.2 %all-gather.8.cloned.1.call-done = bf16[8,256,384]{2,1,0:T(8,128)(2,1)} async-done(((bf16[8,8,384]{2,1,0:T(8,128)(2,1)}), bf16[8,256,384]{2,1,0:T(8,128)(2,1)}) %all-gather.8.cloned.1.call-update) | async-done | bytes 1572880 | tf_op jit(solution)/shard_map/all_gather | solution.py:73
  182.7 2.0 gather_fusion
  184.9 1.4 copy.88
  186.3 2.0 gather_fusion.1
  189.8 179.7 %all-gather.4.cloned.1.call-done = bf16[8192,384]{0,1:T(8,128)(2,1)} async-done(((bf16[256,384]{0,1:T(8,128)(2,1)}), bf16[8192,384]{0,1:T(8,128)(2,1)}) %all-gather.4.cloned.1.call-update) | async-done | bytes 6291472 | tf_op jit(solution)/shard_map/all_gather | solution.py:54
  369.5 185.6 %all-gather.6.cloned.1.call-done = bf16[8192,384]{0,1:T(8,128)(2,1)} async-done(((bf16[256,384]{0,1:T(8,128)(2,1)}), bf16[8192,384]{0,1:T(8,128)(2,1)}) %all-gather.6.cloned.1.call-update) | async-done | bytes 6291472 | tf_op jit(solution)/shard_map/all_gather | solution.py:55
  555.1 47.0 %while.20 = (s32[]{:T(128)}, f32[3,256]{1,0:T(4,128)S(1)}, f32[3,256]{1,0:T(4,128)S(1)}, f32[3,256,128]{2,1,0:T(8,128)S(1)}, pred[2,64]{1,0:T(4,128)(4,1)S(1)}, ...) while((s32[]{:T(128)}, f32[3,256]{1,0:T(4,128)S(1)}, ...), condition=%wide.region_3.4_spmd.clone, body=%wide.region_0.3_spmd.clone.sunk | while | flops 205164320 | bytes 8636838 | solution.py:70
  555.3 1.2 constant_dynamic-slice_fusion.5
  557.3 0.7 convolution_add_fusion.2
  558.2 1.2 constant_dynamic-slice_fusion.5
  561.1 1.2 constant_dynamic-slice_fusion.5
  564.1 1.2 constant_dynamic-slice_fusion.5
  567.0 1.2 constant_dynamic-slice_fusion.5
  570.0 1.2 constant_dynamic-slice_fusion.5
  572.0 0.7 convolution_add_fusion.2
  572.9 1.2 constant_dynamic-slice_fusion.5
  575.9 1.2 constant_dynamic-slice_fusion.5
  578.8 1.2 constant_dynamic-slice_fusion.5
  581.7 1.2 constant_dynamic-slice_fusion.5
  584.7 1.2 constant_dynamic-slice_fusion.5
  587.6 1.2 constant_dynamic-slice_fusion.5
  590.6 1.2 constant_dynamic-slice_fusion.5
  593.5 1.2 constant_dynamic-slice_fusion.5
  596.4 1.2 constant_dynamic-slice_fusion.5
  599.4 1.2 constant_dynamic-slice_fusion.5
  602.4 35.9 %psum.7 = f32[256]{0:T(256)S(1)} all-reduce(f32[256]{0:T(256)S(1)} %get-tuple-element.276), channel_id=1, replica_groups=mesh['seq'=32,'head'=16] {'head'}, use_global_device_ids=true, to_apply=%region_7.8 | all-reduce | flops 256 | bytes 2048 | tf_op jit(solution)/shard_map/psum | solution.py:100
  638.4 0.8 copy.72
  (179 shorter events, 28.2 us)
Async XLA Ops:
  6.5 176.2 %all-gather.8.cloned.1.call-start = ((), (), s32[]{:S(2)}) async-start(), calls=%async_computation.3 | async-start | bytes 1622016 | tf_op jit(solution)/shard_map/all_gather | solution.py:73
  7.3 362.2 %all-gather.4.cloned.1.call-start = ((), (), s32[]{:S(2)}) async-start(), calls=%async_computation.1 | async-start | bytes 6488064 | tf_op jit(solution)/shard_map/all_gather | solution.py:54
  9.1 546.0 %all-gather.6.cloned.1.call-start = ((), (), s32[]{:S(2)}) async-start(), calls=%async_computation.2 | async-start | bytes 6488064 | tf_op jit(solution)/shard_map/all_gather | solution.py:55
  13.1 18.8 %copy-start = (bf16[256,384]{1,0:T(8,128)(2,1)S(1)}, bf16[256,384]{1,0:T(8,128)(2,1)}, u32[]{:S(2)}) copy-start(bf16[256,384]{1,0:T(8,128)(2,1)} %param.10) | copy-start | bytes 589828
  13.1 19.1 %copy-start.1 = (bf16[384]{0:T(512)(128)(2,1)S(1)}, bf16[384]{0:T(512)(128)(2,1)}, u32[]{:S(2)}) copy-start(bf16[384]{0:T(512)(128)(2,1)} %param.17) | copy-start | bytes 2308
  13.1 19.3 %copy-start.3 = (s32[2]{0:T(128)S(1)}, s32[2]{0:T(128)}, u32[]{:S(2)}) copy-start(s32[2]{0:T(128)} %param.14) | copy-start | bytes 28
  13.1 19.3 %copy-start.2 = (s32[2,64]{1,0:T(2,128)S(1)}, s32[2,64]{1,0:T(2,128)}, u32[]{:S(2)}) copy-start(s32[2,64]{1,0:T(2,128)} %param.13) | copy-start | bytes 1540
  13.1 171.8 %all-to-all-start = ((bf16[32,8,8,384]{3,2,1,0:T(8,128)(2,1)}), bf16[32,8,8,384]{3,2,1,0:T(8,128)(2,1)S(1)}, u32[]{:S(2)}, u32[]{:S(2)}) async-start(bf16[32,8,8,384]{3,2,1,0:T(8,128)(2,1)} %stack.2), calls=%async_computation | async-start | bytes 3145728 | tf_op jit(solution)/shard_map/all_to_all | solution.py:14
Sparse Core Ops, SparseCore 0:
  10.3 172.3 all-gather.7
  185.6 183.8 all-gather.3
  372.4 182.6 all-gather.5
